TPU v7x, 512 devices: a whole 4x4x16 slice. The times are simulated.
512 devices in a mesh: blk: 32 (over z_lo, x), grp: 16 (over z_hi, y, core).
Axes of the slice: x: 4, y: 4, z: 16 (z_hi: 2, z_lo: 8; z = z_hi * 8 + z_lo), core: 2. Of those that a mesh axis runs over, the one named last changes fastest.
Arguments:
- positions: float32 [3, 32768], P(None, ('blk', 'grp')), may hold values from -0.25 to 31.25, as said below
- moments: float32 [2, 2, 3, 32768], P(None, None, None, ('blk', 'grp')), may hold values from -6 to 6
- inv_polar_re: float32 [32768], P(('blk', 'grp')), may hold values from 0.5 to 2
- inv_polar_im: float32 [32768], P(('blk', 'grp')), may hold values from -0.5 to 0.5
- mode_field: float32 [2, 3, 32768, 512], P(None, None, ('blk', 'grp')), may hold values from -0.0390625 to 0.0390625
- mode_detune: float32 [512], replicated, may hold values from -1 to 1
- mode_width: float32 [512], replicated, may hold values from 0.05 to 1
Outputs:
- response: float32 [2, 2, 3, 32768], P(None, None, None, ('blk', 'grp'))
Inputs may be any that keep to these rules, and one draw needn't show every extreme that they name: `positions`: dipole n lies within 0.25, in each coordinate, of the lattice site (n % 32, (n // 32) % 32, n // 1024); distinct dipoles are at least 0.5 apart.
All inputs are finite; a program needn't handle non-finite values.
Results may differ from a plain program's by a relative error of at most 0.0003.
Values sent between devices are 32-bit elements; how exact they have to be, the bound alone decides.
A program may use at most 64 MiB of HBM per device.

v0:
```python
import math

import jax
import jax.numpy as jnp
from jax import lax
from jax.sharding import Mesh
from jax.sharding import PartitionSpec as P

BLK_GRP = ("blk_0", "blk_1", "grp_0", "grp_1", "grp_2")
GRP = ("grp_0", "grp_1", "grp_2")
BLK = ("blk_0", "blk_1")


wavenumber = 1.0
coupling = 0.05
near_limit = 0.04


def over_axes(value, axes):
    for axis in axes:
        value = lax.psum(value, axis)
    return value


def laid_out(tiles, dim):
    tiles = jnp.moveaxis(tiles, 0, dim)
    shape = tiles.shape
    return tiles.reshape(*shape[:dim], shape[dim] * shape[dim + 1], *shape[dim + 2 :])


def gather_in_order(value, axes, sequence):
    tiles = value[None]
    for k in sequence:
        tiles = lax.all_gather(tiles, axes[k], axis=0, tiled=True)
    block = [lax.axis_size(axes[k]) for k in reversed(sequence)]
    tiles = tiles.reshape(*block, *value.shape)
    turned = sorted(range(len(sequence)), key=lambda place: sequence[len(sequence) - 1 - place])
    return tiles.transpose(*turned, *range(len(sequence), tiles.ndim)).reshape(-1, *value.shape)


def whole_of(value, axes, sequence, dim):
    return laid_out(gather_in_order(value, axes, sequence), dim)


def sent_to_all(value, axis):
    devices = lax.axis_size(axis)
    return lax.all_to_all(
        jnp.broadcast_to(value[None], (devices, *value.shape)), axis, 0, 0, tiled=True
    )


def gather_directly(value, axis, dim):
    return laid_out(sent_to_all(value, axis), dim)


def sent_together(arrays, axis, dim, along):
    ends, at = ([], 0)
    for a in arrays[:-1]:
        at += a.shape[along]
        ends.append(at)
    both = jnp.concatenate(arrays, axis=along)
    return tuple(jnp.split(gather_directly(both, axis, dim), ends, axis=along))


def cut_along(value, dim, devices):
    before, after = (value.shape[:dim], value.shape[dim + 1 :])
    return jnp.moveaxis(value.reshape(*before, devices, -1, *after), dim, 0)


def sent_and_summed(value, axis, dim):
    tiles = cut_along(value, dim, lax.axis_size(axis))
    arrived = lax.all_to_all(tiles, axis, split_axis=0, concat_axis=0, tiled=True)
    return arrived.sum(axis=0)


def pair_field(deltas, dipoles, axis_sum):
    delta_x, delta_y, delta_z = deltas
    square = delta_x * delta_x + delta_y * delta_y + delta_z * delta_z
    coincide = square < near_limit
    safe_square = jnp.where(coincide, 1.0, square)
    inverse = 1.0 / jnp.sqrt(safe_square)
    phase_arg = wavenumber * safe_square * inverse
    cos_val = jnp.cos(phase_arg)
    sine_val = jnp.sin(phase_arg)
    masked_cube = jnp.where(coincide, 0.0, inverse * inverse * inverse)
    near_re = phase_arg * phase_arg - 1.0
    far_re = 3.0 - phase_arg * phase_arg
    diag_re = (cos_val * near_re - sine_val * phase_arg) * masked_cube
    diag_im = (sine_val * near_re + cos_val * phase_arg) * masked_cube
    scaled = masked_cube / safe_square
    outer_re = (cos_val * far_re + 3.0 * sine_val * phase_arg) * scaled
    outer_im = (sine_val * far_re - 3.0 * cos_val * phase_arg) * scaled
    tile_list = []
    for drive_set in range(len(dipoles) // 6):
        moment_re = dipoles[6 * drive_set : 6 * drive_set + 3]
        moment_im = dipoles[6 * drive_set + 3 : 6 * drive_set + 6]
        proj_re = delta_x * moment_re[0] + delta_y * moment_re[1] + delta_z * moment_re[2]
        proj_im = delta_x * moment_im[0] + delta_y * moment_im[1] + delta_z * moment_im[2]
        along_re = outer_re * proj_re - outer_im * proj_im
        along_im = outer_re * proj_im + outer_im * proj_re
        for component in range(3):
            tile_list.append(
                diag_re * moment_re[component]
                - diag_im * moment_im[component]
                + deltas[component] * along_re
            )
        for component in range(3):
            tile_list.append(
                diag_re * moment_im[component]
                + diag_im * moment_re[component]
                + deltas[component] * along_im
            )
    return jnp.stack([jnp.sum(entry_tile, axis=axis_sum) for entry_tile in tile_list])


def contract(left, right):
    return lax.dot_general(left, right, (((0,), (1,)), ((), ())), precision=lax.Precision.HIGHEST)


def modal_project(mode_rows, moment_rows):
    amp_re = contract(mode_rows[0], moment_rows[:, 0]) - contract(mode_rows[1], moment_rows[:, 1])
    amp_im = contract(mode_rows[0], moment_rows[:, 1]) + contract(mode_rows[1], moment_rows[:, 0])
    return (amp_re, amp_im)


def spread(weights, rows):
    return lax.dot_general(weights, rows, (((0,), (1,)), ((), ())), precision=lax.Precision.HIGHEST)


def modal_spread(mode_rows, amp_re, amp_im, mode_detune, mode_width):
    denominator = mode_detune * mode_detune + mode_width * mode_width
    resp_re = (mode_detune / denominator)[:, None]
    resp_im = (mode_width / denominator)[:, None]
    weighted_re = resp_re * amp_re - resp_im * amp_im
    weighted_im = resp_re * amp_im + resp_im * amp_re
    out_re = spread(weighted_re, mode_rows[0]) - spread(weighted_im, mode_rows[1])
    out_im = spread(weighted_re, mode_rows[1]) + spread(weighted_im, mode_rows[0])
    return jnp.stack([out_re, out_im], axis=1)


def combine(moments, inv_polar_re, inv_polar_im, pair_part, modal_part):
    drives = moments.shape[0]
    dipole_count = moments.shape[3]
    field_sum = coupling * pair_part.reshape(drives, 2, 3, dipole_count) + modal_part.reshape(
        drives, 2, 3, dipole_count
    )
    moment_re = moments[:, 0]
    moment_im = moments[:, 1]
    resp_re = inv_polar_re * moment_re - inv_polar_im * moment_im - field_sum[:, 0]
    resp_im = inv_polar_re * moment_im + inv_polar_im * moment_re - field_sum[:, 1]
    return jnp.stack([resp_re, resp_im], axis=1)


def on_device(positions, moments, inv_polar_re, inv_polar_im, mode_field, mode_detune, mode_width):
    drives = moments.shape[0]
    dipole_count = positions.shape[1]
    flat_moments = moments.reshape(drives * 6, dipole_count)
    mode_rows = mode_field.reshape(2, 3 * dipole_count, mode_field.shape[3])
    amp_re, amp_im = modal_project(mode_rows, moments.reshape(drives, 2, 3 * dipole_count))
    amp_re, amp_im = (over_axes(amp_re, BLK_GRP), over_axes(amp_im, BLK_GRP))
    modal_part = modal_spread(mode_rows, amp_re, amp_im, mode_detune, mode_width).reshape(
        drives * 6, dipole_count
    )
    group_pos = whole_of(positions, (("grp_0", "grp_1"), "grp_2"), (0, 1), 1)
    initial = jnp.zeros((drives * 6, group_pos.shape[1]), jnp.float32)
    places, dipoles = sent_together((positions, flat_moments), BLK, 1, 0)
    columns = places.shape[1]
    block_width = math.gcd(columns, 256)

    def advance(block, inner):
        source_pos = lax.dynamic_slice_in_dim(places, block * block_width, block_width, 1)
        source_mom = lax.dynamic_slice_in_dim(dipoles, block * block_width, block_width, 1)
        deltas = [group_pos[axis_c][None, :] - source_pos[axis_c][:, None] for axis_c in range(3)]
        return inner + pair_field(
            deltas, [source_mom[member][:, None] for member in range(drives * 6)], 0
        )

    partial_value = lax.fori_loop(0, columns // block_width, advance, initial)
    pair_part = sent_and_summed(partial_value, GRP, 1)
    return combine(moments, inv_polar_re, inv_polar_im, pair_part, modal_part)


def solution(mesh):
    torus = Mesh(mesh.devices.reshape(8, 4, 2, 4, 2), ("blk_0", "blk_1", "grp_0", "grp_1", "grp_2"))
    placed = (
        P(None, BLK_GRP),
        P(None, None, None, BLK_GRP),
        P(BLK_GRP),
        P(BLK_GRP),
        P(None, None, BLK_GRP, None),
        P(),
        P(),
    )
    return jax.shard_map(
        on_device,
        mesh=torus,
        in_specs=placed,
        out_specs=P(None, None, None, BLK_GRP),
        check_vma=False,
    )
```

profile of v0, /device:TPU:1, one launch (start us, length us, event | category | flops | bytes accessed | tf_op | source)
XLA Modules:
  0.0 260.5 jit_solution(8766813554993038770)
XLA Ops:
  0.0 0.8 copy.39
  0.8 0.7 pad_maximum_fusion
  1.5 0.8 reshape.63
  2.3 15.9 %all-to-all-start = ((f32[32,1,960]{2,1,0:T(1,128)}), f32[32,1,960]{2,1,0:T(1,128)S(1)}, u32[]{:S(2)}, u32[]{:S(2)}) async-start(f32[32,1,960]{2,1,0:T(1,128)} %reshape.63), calls=%async_computation | async-start | bytes 262144 | tf_op jit(solution)/shard_map/all_to_all | solution.py:47
  18.4 0.3 fusion.49
  18.8 0.3 fusion.53
  19.1 0.3 convolution_add_fusion
  19.4 0.3 convolution_subtract_fusion
  19.7 29.8 %all-reduce = (f32[512,2]{0,1:T(2,128)S(1)}, f32[512,2]{0,1:T(2,128)S(1)}) all-reduce(f32[512,2]{0,1:T(2,128)S(1)} %convolution_add_fusion, f32[512,2]{0,1:T(2,128)S(1)} %convolution_subtract_fusion), channel_id=1, replica_groups=mesh['blk_0'=8,'blk_1'=4,'grp_0'=2,'grp_1'=4,'grp_2'=2] {'blk_0'}, use_global_device_ids=true, to_apply=%region_20.0 | all-reduce | flops 2048 | bytes 16384 | tf_op jit(solution)/shard_map/psum | solution.py:21
  49.5 8.5 %all-reduce.2 = (f32[512,2]{0,1:T(2,128)S(1)}, f32[512,2]{0,1:T(2,128)S(1)}) all-reduce(f32[512,2]{0,1:T(2,128)S(1)} %get-tuple-element.184, f32[512,2]{0,1:T(2,128)S(1)} %get-tuple-element.185), channel_id=1, replica_groups=mesh['blk_0'=8,'blk_1'=4,'grp_0'=2,'grp_1'=4,'grp_2'=2] {'blk_1'}, use_global_device_ids=true, to_apply=%region_21.0 | all-reduce | flops 2048 | bytes 16384 | tf_op jit(solution)/shard_map/psum | solution.py:21
  58.1 12.6 %all-reduce.4 = (f32[512,2]{0,1:T(2,128)S(1)}, f32[512,2]{0,1:T(2,128)S(1)}) all-reduce(f32[512,2]{0,1:T(2,128)S(1)} %get-tuple-element.188, f32[512,2]{0,1:T(2,128)S(1)} %get-tuple-element.189), channel_id=1, replica_groups=mesh['blk_0'=8,'blk_1'=4,'grp_0'=2,'grp_1'=4,'grp_2'=2] {'grp_0'}, use_global_device_ids=true, to_apply=%region_22.0 | all-reduce | flops 2048 | bytes 16384 | tf_op jit(solution)/shard_map/psum | solution.py:21
  70.6 9.1 %all-reduce.1 = (f32[512,2]{0,1:T(2,128)S(1)}, f32[512,2]{0,1:T(2,128)S(1)}) all-reduce(f32[512,2]{0,1:T(2,128)S(1)} %get-tuple-element.192, f32[512,2]{0,1:T(2,128)S(1)} %get-tuple-element.193), channel_id=1, replica_groups=mesh['blk_0'=8,'blk_1'=4,'grp_0'=2,'grp_1'=4,'grp_2'=2] {'grp_1'}, use_global_device_ids=true, to_apply=%region_23.24 | all-reduce | flops 2048 | bytes 16384 | tf_op jit(solution)/shard_map/psum | solution.py:21
  79.8 12.2 %all-reduce.3 = (f32[512,2]{0,1:T(2,128)S(1)}, f32[512,2]{0,1:T(2,128)S(1)}) all-reduce(f32[512,2]{0,1:T(2,128)S(1)} %get-tuple-element.186, f32[512,2]{0,1:T(2,128)S(1)} %get-tuple-element.187), channel_id=1, replica_groups=mesh['blk_0'=8,'blk_1'=4,'grp_0'=2,'grp_1'=4,'grp_2'=2] {'grp_2'}, use_global_device_ids=true, to_apply=%region_24.25 | all-reduce | flops 2048 | bytes 16384 | tf_op jit(solution)/shard_map/psum | solution.py:21
  92.0 0.4 fusion.62
  92.4 0.4 convolution_subtract_fusion.1
  92.9 0.1 stack.144
  93.0 0.2 copy-done.1
  93.1 53.9 %all-gather.1 = f32[8,3,64]{2,1,0:T(4,128)S(1)} all-gather(f32[1,3,64]{2,1,0:T(4,128)S(1)} %bitcast.166), channel_id=2, replica_groups=mesh['blk_0'=8,'blk_1'=4,'grp_0'=2,'grp_1'=4,'grp_2'=2] {'grp_0','grp_1'}, dimensions={0}, use_global_device_ids=true | all-gather | bytes 6912 | tf_op jit(solution)/shard_map/all_gather | solution.py:34
  147.0 6.4 %all_gather.7 = f32[16,3,64]{2,0,1:T(8,128)S(1)} all-gather(f32[8,3,64]{2,0,1:T(8,128)S(1)} %copy.41), channel_id=1, replica_groups=mesh['blk_0'=8,'blk_1'=4,'grp_0'=2,'grp_1'=4,'grp_2'=2] {'grp_2'}, dimensions={0}, use_global_device_ids=true | all-gather | bytes 18432 | tf_op jit(solution)/shard_map/all_gather | solution.py:34
  153.6 0.4 fusion.61
  154.0 0.6 broadcast.270
  154.6 0.9 reduce
  155.7 0.1 split.13
  155.9 79.1 %while.16 = (s32[]{:T(128)}, f32[12,1024]{1,0:T(8,128)S(1)}, f32[3,1024]{1,0:T(4,128)S(1)}, f32[3,2048]{1,0:T(4,128)S(1)}, f32[12,2048]{1,0:T(8,128)S(1)}, /*ind...) while((s32[]{:T(128)}, f32[12,1024]{1,0:T(8,128)S(1)}, ...), condition=%wide.region_13.0_spmd.clone, body=%wide.region_0.13_spmd.clone.sunk | while | flops 36712464 | bytes 378273 | solution.py:178
  156.0 0.1 constant_dynamic-slice_fusion.3
  156.1 9.6 %fusion.77 = (f32[1024]{0:T(1024)S(1)}, f32[1024]{0:T(1024)S(1)}, f32[1024]{0:T(1024)S(1)}, f32[1024]{0:T(1024)S(1)}, f32[1024]{0:T(1024)S(1)}, /*index=5*/f32[1...) fusion(f32[256]{0:T(256)S(1)} %bitcast.160, ...), kind=kLoop, calls=%fused_computation.76.clone.1 | loop fusion | flops 36687872 | bytes 76800 | tf_op jit(solution)/shard_map/while/body/eval_jaxpr/reduce_sum | solution.py:113
  165.8 0.1 constant_dynamic-slice_fusion.3
  166.0 9.6 %fusion.77 = (f32[1024]{0:T(1024)S(1)}, f32[1024]{0:T(1024)S(1)}, f32[1024]{0:T(1024)S(1)}, f32[1024]{0:T(1024)S(1)}, f32[1024]{0:T(1024)S(1)}, /*index=5*/f32[1...) fusion(f32[256]{0:T(256)S(1)} %bitcast.160, ...), kind=kLoop, calls=%fused_computation.76.clone.1 | loop fusion | flops 36687872 | bytes 76800 | tf_op jit(solution)/shard_map/while/body/eval_jaxpr/reduce_sum | solution.py:113
  175.6 0.1 stack.162
  175.7 0.1 constant_dynamic-slice_fusion.3
  175.9 9.6 %fusion.77 = (f32[1024]{0:T(1024)S(1)}, f32[1024]{0:T(1024)S(1)}, f32[1024]{0:T(1024)S(1)}, f32[1024]{0:T(1024)S(1)}, f32[1024]{0:T(1024)S(1)}, /*index=5*/f32[1...) fusion(f32[256]{0:T(256)S(1)} %bitcast.160, ...), kind=kLoop, calls=%fused_computation.76.clone.1 | loop fusion | flops 36687872 | bytes 76800 | tf_op jit(solution)/shard_map/while/body/eval_jaxpr/reduce_sum | solution.py:113
  185.6 0.1 constant_dynamic-slice_fusion.3
  185.8 9.6 %fusion.77 = (f32[1024]{0:T(1024)S(1)}, f32[1024]{0:T(1024)S(1)}, f32[1024]{0:T(1024)S(1)}, f32[1024]{0:T(1024)S(1)}, f32[1024]{0:T(1024)S(1)}, /*index=5*/f32[1...) fusion(f32[256]{0:T(256)S(1)} %bitcast.160, ...), kind=kLoop, calls=%fused_computation.76.clone.1 | loop fusion | flops 36687872 | bytes 76800 | tf_op jit(solution)/shard_map/while/body/eval_jaxpr/reduce_sum | solution.py:113
  195.5 0.1 constant_dynamic-slice_fusion.3
  195.6 9.6 %fusion.77 = (f32[1024]{0:T(1024)S(1)}, f32[1024]{0:T(1024)S(1)}, f32[1024]{0:T(1024)S(1)}, f32[1024]{0:T(1024)S(1)}, f32[1024]{0:T(1024)S(1)}, /*index=5*/f32[1...) fusion(f32[256]{0:T(256)S(1)} %bitcast.160, ...), kind=kLoop, calls=%fused_computation.76.clone.1 | loop fusion | flops 36687872 | bytes 76800 | tf_op jit(solution)/shard_map/while/body/eval_jaxpr/reduce_sum | solution.py:113
  205.4 0.1 constant_dynamic-slice_fusion.3
  205.5 9.6 %fusion.77 = (f32[1024]{0:T(1024)S(1)}, f32[1024]{0:T(1024)S(1)}, f32[1024]{0:T(1024)S(1)}, f32[1024]{0:T(1024)S(1)}, f32[1024]{0:T(1024)S(1)}, /*index=5*/f32[1...) fusion(f32[256]{0:T(256)S(1)} %bitcast.160, ...), kind=kLoop, calls=%fused_computation.76.clone.1 | loop fusion | flops 36687872 | bytes 76800 | tf_op jit(solution)/shard_map/while/body/eval_jaxpr/reduce_sum | solution.py:113
  215.3 0.1 constant_dynamic-slice_fusion.3
  215.4 9.6 %fusion.77 = (f32[1024]{0:T(1024)S(1)}, f32[1024]{0:T(1024)S(1)}, f32[1024]{0:T(1024)S(1)}, f32[1024]{0:T(1024)S(1)}, f32[1024]{0:T(1024)S(1)}, /*index=5*/f32[1...) fusion(f32[256]{0:T(256)S(1)} %bitcast.160, ...), kind=kLoop, calls=%fused_computation.76.clone.1 | loop fusion | flops 36687872 | bytes 76800 | tf_op jit(solution)/shard_map/while/body/eval_jaxpr/reduce_sum | solution.py:113
  225.1 0.1 constant_dynamic-slice_fusion.3
  225.3 9.6 %fusion.77 = (f32[1024]{0:T(1024)S(1)}, f32[1024]{0:T(1024)S(1)}, f32[1024]{0:T(1024)S(1)}, f32[1024]{0:T(1024)S(1)}, f32[1024]{0:T(1024)S(1)}, /*index=5*/f32[1...) fusion(f32[256]{0:T(256)S(1)} %bitcast.160, ...), kind=kLoop, calls=%fused_computation.76.clone.1 | loop fusion | flops 36687872 | bytes 76800 | tf_op jit(solution)/shard_map/while/body/eval_jaxpr/reduce_sum | solution.py:113
  235.1 0.7 reshape.65
  235.9 7.9 %all-to-all-start.1 = ((f32[16,1,768]{2,1,0:T(1,128)}), f32[16,1,768]{2,1,0:T(1,128)S(1)}, u32[]{:S(2)}, u32[]{:S(2)}) async-start(f32[16,1,768]{2,1,0:T(1,128)} %reshape.65), calls=%async_computation.1 | async-start | bytes 98304 | tf_op jit(solution)/shard_map/all_to_all | solution.py:72
  243.8 0.4 convolution_add_fusion.1
  244.3 14.0 %all-to-all-done.1 = f32[16,1,768]{2,1,0:T(1,128)S(1)} async-done(((f32[16,1,768]{2,1,0:T(1,128)}), f32[16,1,768]{2,1,0:T(1,128)S(1)}, u32[]{:S(2)}, u32[]{:S(2)}) %all-to-all-start.1) | async-done | bytes 49184 | tf_op jit(solution)/shard_map/all_to_all | solution.py:72
  258.3 0.7 reduce.1
  259.3 0.6 copy-done.4
  259.9 0.6 copy.50
  (60 shorter events, 1.9 us)
Async XLA Ops:
  0.0 18.3 %copy-start = (f32[2,3,64,512]{3,2,1,0:T(8,128)S(1)}, f32[2,3,64,512]{3,2,1,0:T(8,128)}, u32[]{:S(2)}) copy-start(f32[2,3,64,512]{3,2,1,0:T(8,128)} %param.13) | copy-start | bytes 2359300
  2.3 151.6 %all-to-all-start = ((f32[32,1,960]{2,1,0:T(1,128)}), f32[32,1,960]{2,1,0:T(1,128)S(1)}, u32[]{:S(2)}, u32[]{:S(2)}) async-start(f32[32,1,960]{2,1,0:T(1,128)} %reshape.63), calls=%async_computation | async-start | bytes 262144 | tf_op jit(solution)/shard_map/all_to_all | solution.py:47
  79.8 12.2 %copy-start.2 = (f32[512]{0:T(512)S(1)}, f32[512]{0:T(512)}, u32[]{:S(2)}) copy-start(f32[512]{0:T(512)} %param.14) | copy-start | bytes 6148
  79.8 12.2 %copy-start.3 = (f32[512]{0:T(512)S(1)}, f32[512]{0:T(512)}, u32[]{:S(2)}) copy-start(f32[512]{0:T(512)} %param.15) | copy-start | bytes 6148
  92.4 0.7 copy-start.1
  235.9 22.5 %all-to-all-start.1 = ((f32[16,1,768]{2,1,0:T(1,128)}), f32[16,1,768]{2,1,0:T(1,128)S(1)}, u32[]{:S(2)}, u32[]{:S(2)}) async-start(f32[16,1,768]{2,1,0:T(1,128)} %reshape.65), calls=%async_computation.1 | async-start | bytes 98304 | tf_op jit(solution)/shard_map/all_to_all | solution.py:72
  259.2 0.7 copy-start.4
  259.3 0.7 copy-start.5
where the time goes:
time: 261 us
  blocking collectives  133 us (51%)
  other arithmetic  79.1 us (30%)
  starting transfers between devices  23.9 us (9%)
  waiting for transfers between devices  14 us (5%)
  local copies, waits for them, and re-layouts  7.4 us (3%)
  matrix products  2.91 us (1%)
    reduce_sum x8, other arithmetic, pair_field(): jnp.sum(entry_tile, axis=axis_sum)  76.6 us
    psum x5, blocking collectives, over_axes(): value = lax.psum(value, axis)  72.2 us
    all_gather x2, blocking collectives, gather_in_order(): tiles = lax.all_gather(tiles, axes[k], axis=0, tiled=True)  60.3 us
    all_to_all x1, starting transfers between devices, sent_to_all(): lax.all_to_all(jnp.broadcast_to(value[None], (devices, *value.shape)), ax...  15.9 us
    all_to_all x1, waiting for transfers between devices, sent_and_summed(): lax.all_to_all(tiles, axis, split_axis=0, concat_axis=0, tiled=True)  14 us
    all_to_all x1, starting transfers between devices, sent_and_summed(): lax.all_to_all(tiles, axis, split_axis=0, concat_axis=0, tiled=True)  7.95 us
  transfers between devices with their start and end apart: 2, of which 1 were waited for; matrix products, arithmetic and copies ran while one was open for 1% of the time, Pallas kernels for 0%

commit v1 on v0

v1 whole, which is shorter than its diff:
```python
import math

import jax
import jax.numpy as jnp
import numpy as np
from jax import lax
from jax.experimental import pallas as pl
from jax.experimental.pallas import tpu as pltpu
from jax.sharding import PartitionSpec as P

F32, BF16 = jnp.float32, jnp.bfloat16
MESH = pl.DeviceIdType.MESH
KAPPA = 1.0 / (2.0 * math.pi)
COUPLING = 0.05
SHIFT = 1.25
HUGE = 1e30


def feature_maps():
    e = np.zeros((4, 160, 96), np.float32)
    for c in range(4):
        delta = (c - 1.5) * SHIFT
        base = np.zeros((160, 32), np.float32)
        for d in range(2):
            for j in range(15):
                row = j * 2 + d
                if j < 3:
                    base[row, 3] = 1.0; comp = j
                elif j < 12:
                    a, comp = divmod(j - 3, 3)
                else:
                    a, comp = j - 12, None
                if j >= 3:
                    base[row, a] = 1.0
                    if a == 0: base[row, 3] = -delta
                for ri in range(2):
                    m = 4 + d * 6 + ri * 3
                    if comp is not None:
                        base[32 + 32 * ri + row, m + comp] = -3.0
                    else:
                        base[32 + 32 * ri + row, 16 + d * 2 + ri] = -3.0
                        base[32 + 32 * ri + row, m] = 3.0 * delta
                        base[96 + 32 * ri + row, m + a] = 1.0
        for piece in range(3):
            e[c, :, 32 * piece:32 * piece + 32] = base
    return e


def pieces(v):
    h = v.astype(BF16).astype(F32)
    rest = v - h
    m = rest.astype(BF16).astype(F32)
    return h, m, rest - m


S4 = [4.442882834891087, -7.308241184594817, 3.6062893302761356, -0.8457653963567059, 0.10920874208169386]
C5 = [1.4142134965690698, -6.978850988398392, 5.73946117217025, -1.8835629909695983, 0.3106981907767927]

def planes(r2):
    y = lax.rsqrt(r2)
    w = r2 * y
    f = w - jnp.round(w)
    t = f * f
    s = S4[-1]
    for k in S4[-2::-1]: s = s * t + k
    s = s * f
    c = C5[-1]
    for k in C5[-2::-1]: c = c * t + k
    sy = s * y
    gr = y - s * sy
    gi = sy * c
    q = y * y
    u = y * KAPPA
    v1 = 1.0 - q * (KAPPA * KAPPA)
    ar = gr * v1 - gi * u
    ai = gi * v1 + gr * u
    br = q * (ar - (2.0 / 3.0) * gr)
    bi = q * (ai - (2.0 / 3.0) * gi)
    return ar, ai, br, bi


def split(v):
    h = v.astype(BF16)
    return h, (v - h.astype(F32)).astype(BF16)


def perm_map():
    m = np.zeros((64, 128), np.float32)
    for r in range(2):
        for c in range(4):
            for x in range(8):
                m[32 * r + 8 * c + x, 16 * c + 8 * r + x] = 1.0
    m[:, 64:] = m[:, :64]
    return m


def prep_targets(tpos, o_t, tag_dev, ta, xrow):
    lane8 = lax.broadcasted_iota(jnp.int32, (8, 128), 1)
    lane = lax.broadcasted_iota(jnp.int32, (8, 256), 1)
    sub = lax.broadcasted_iota(jnp.int32, (8, 256), 0)
    org = jnp.where(sub == 0, o_t[0], jnp.where(sub == 1, o_t[1], o_t[2]))
    jrow = lax.broadcasted_iota(jnp.int32, (64, 256), 0)
    jlane = lax.broadcasted_iota(jnp.int32, (64, 256), 1)
    for c in range(4):
        halves = []
        for t in range(2):
            v = jnp.zeros((8, 128), F32)
            for k in range(8):
                shift = (16 * (k - c)) % 128
                a = tpos[8 * t + k]
                if shift: a = pltpu.roll(a, shift, 1)
                v = jnp.where(lane8 // 16 == k, a, v)
            halves.append(v)
        raw = jnp.concatenate(halves, axis=1)
        delta = (c - 1.5) * SHIFT
        loc = (raw - org) * KAPPA - jnp.where(sub == 0, delta, 0.0)
        loc = jnp.where(sub < 3, loc, 0.0)
        xrow[c] = loc
        n2 = jnp.sum(loc * loc, axis=0, keepdims=True)
        v = jnp.where(sub == c, -2.0 * loc[0:1], jnp.where(sub == 4, -2.0 * loc[1:2], jnp.where(sub == 5, -2.0 * loc[2:3], jnp.where(sub == 6, n2, 0.0))))
        h, m, l = pieces(v)
        g6 = jnp.where((sub == c) | (sub == 4 + c), 1.0, 0.0)
        g7 = jnp.where(sub == c, 1.0, 0.0)
        tag = jnp.where((jlane // 16 == tag_dev) & (jrow == 16 * c + jlane % 16), HUGE, 0.0)
        ta[c] = jnp.concatenate([h, m, l, h, m, h, g6, g7, tag], axis=0).astype(BF16)


def prep_sources(src, slot, o_s, oy_r2, own_tag, emap, wmat, sb):
    low = lax.broadcasted_iota(jnp.int32, (8, 128), 1) < 64
    ra, rb = [], []
    for p in range(2):
        a, b = src[4 * slot + 2 * p], src[4 * slot + 2 * p + 1]
        ra.append(jnp.where(low, a, pltpu.roll(b, 64, 1)))
        rb.append(jnp.where(low, pltpu.roll(a, 64, 1), b))
    fa = jnp.concatenate(ra, axis=1)
    fb = jnp.concatenate(rb, axis=1)
    sub = lax.broadcasted_iota(jnp.int32, (8, 256), 0)
    org = jnp.where(sub == 0, o_s[0], jnp.where(sub == 1, o_s[1], o_s[2]))
    loc = (fa - org) * KAPPA
    yr2 = (fa[1:2] - oy_r2) * KAPPA
    f0 = jnp.where(sub < 3, loc, jnp.where(sub == 3, 1.0, fa))
    xs = [f0[k:k + 1] for k in range(3)]
    mom = [f0[4 + k:5 + k] for k in range(4)] + [fb[k:k + 1] for k in range(8)]
    us = []
    for d in range(2):
        for ri in range(2):
            b = d * 6 + ri * 3
            us.append(xs[0] * mom[b] + xs[1] * mom[b + 1] + xs[2] * mom[b + 2])
    f2 = jnp.concatenate(us + [jnp.zeros((4, 256), F32)], axis=0)
    feats = jnp.concatenate([f0, fb, f2, jnp.zeros((8, 256), F32)], axis=0)
    h, m, l = pieces(feats)
    frp = jnp.concatenate([h, m, l], axis=0).astype(BF16)
    for c in range(4):
        o = jnp.dot(emap[c], frp, preferred_element_type=F32)
        xe = o[:32]
        pr, pi = o[32:64] * xe, o[64:96] * xe
        ar, ai = o[96:128], o[128:160]
        for k, (re, im) in enumerate(((ar, ai), (pr, pi))):
            rh, rl = split(re); ih, il = split(im)
            wmat[c, :, pl.ds(512 * k, 256)] = jnp.concatenate([rh, ih, rl, il], axis=0)
            wmat[c, :, pl.ds(512 * k + 256, 256)] = jnp.concatenate([-ih, rh, -il, rl], axis=0)
    lane = lax.broadcasted_iota(jnp.int32, (64, 256), 1)
    j = lax.broadcasted_iota(jnp.int32, (64, 256), 0)
    tag = jnp.where(lane == own_tag + j, 1.0, 0.0)
    shift = (sub.astype(F32) - 1.5) * SHIFT
    va = jnp.where(sub < 4, xs[0] - shift, jnp.where(sub == 4, yr2, jnp.where(sub == 5, xs[2], jnp.where(sub == 6, 1.0, 0.0))))
    yz = yr2 * yr2 + xs[2] * xs[2]
    vb = jnp.where(sub < 4, va * va + yz, 0.0)
    ah, am, al = pieces(va); bh, bm, bl = pieces(vb)
    b6 = jnp.where(sub < 4, bh, pltpu.roll(bm, 4, 0))
    rows = jnp.concatenate([ah, ah, ah, am, am, al, b6, bl, tag], axis=0)
    sb[...] = jnp.concatenate([rows[:, :128].T, rows[:, 128:].T], axis=0).astype(BF16)


def finish(acc, xr, dy):
    t = acc[:64] + acc[64:]
    x = [xr[k:k + 1] for k in range(3)]
    x[1] = x[1] + dy
    out = [None] * 12
    for ri in range(2):
        row = lambda j: t[ri * 32 + 2 * j:ri * 32 + 2 * j + 2]
        s1 = [row(k) for k in range(3)]
        s2 = [[row(3 + 3 * a + k) for k in range(3)] for a in range(3)]
        s3 = [row(12 + k) for k in range(3)]
        inner = x[0] * s1[0] + x[1] * s1[1] + x[2] * s1[2] - (s2[0][0] + s2[1][1] + s2[2][2])
        for c in range(3):
            val = s3[c] + x[c] * inner - (x[0] * s2[c][0] + x[1] * s2[c][1] + x[2] * s2[c][2])
            for d in range(2):
                out[d * 6 + ri * 3 + c] = val[d:d + 1]
    return jnp.concatenate(out, axis=0)


def nn(a, b):
    return lax.dot_general(a, b, (((1,), (0,)), ((), ())), precision=lax.Precision.HIGHEST, preferred_element_type=F32)


def nt(a, b):
    return lax.dot_general(a, b, (((1,), (1,)), ((), ())), precision=lax.Precision.HIGHEST, preferred_element_type=F32)


def permuted(rows, table):
    h, m, l = pieces(rows)
    n = rows.shape[0]
    o = jnp.dot(jnp.concatenate([h, m, l], axis=0).astype(BF16), table, preferred_element_type=F32)
    return o[:n] + o[n : 2 * n] + o[2 * n :]


def kernel(pos, mom, ipr, ipi, mode, det, wid, emap, perm, unperm, out,
           src, tgt, ta, xrow, wmat, sb, g, r2b, acc, amp, rs, zb, cb, ag, obuf, rbuf,
           tgt_s, tgt_r, src_s, src_r, fwd_s, fwd_r, rs_s, rs_r, zb_s, zb_r, cb_s, cb_r, ag_s, ag_r, o_s, o_r):
    blk, grp = lax.axis_index("blk"), lax.axis_index("grp")
    zl, x, zh, y, core = blk // 4, blk % 4, grp // 8, (grp // 2) % 4, grp % 2
    me_r, me_z = x * 4 + y, zh * 8 + zl

    def at_r(r):
        return (zl * 4 + r // 4, zh * 8 + (r % 4) * 2 + core)

    def at_z(z):
        return ((z % 8) * 4 + x, (z // 8) * 8 + y * 2 + core)

    sibling = (blk, zh * 8 + y * 2 + (1 - core))

    barrier = pltpu.get_barrier_semaphore()

    def greet(s, _):
        pl.semaphore_signal(barrier, inc=1, device_id=at_r((me_r + s) % 16), device_id_type=MESH)
        pl.semaphore_signal(barrier, inc=1, device_id=at_z((me_z + s) % 16), device_id_type=MESH)
        return 0

    lax.fori_loop(1, 16, greet, 0)
    pl.semaphore_signal(barrier, inc=1, device_id=sibling, device_id_type=MESH)

    def remote(a, b, ss, rr, dev):
        return pltpu.make_async_remote_copy(src_ref=a, dst_ref=b, send_sem=ss, recv_sem=rr, device_id=dev, device_id_type=MESH)

    def spread_to(buf, ss, rr, me, where):
        def go(s, _):
            j = (me + s) % 16
            remote(buf.at[me], buf.at[me], ss.at[j], rr.at[me], where(j)).start()
            return 0
        lax.fori_loop(1, 16, go, 0)

    def arrived(buf, ss, rr, me, where):
        def go(s, _):
            j = (me + s) % 16
            remote(buf.at[j], buf.at[j], ss.at[j], rr.at[j], where(j)).wait_recv()
            return 0
        lax.fori_loop(1, 16, go, 0)

    def sent(buf, ss, rr, me, where):
        def go(s, _):
            j = (me + s) % 16
            remote(buf.at[me], buf.at[me], ss.at[j], rr.at[me], where(j)).wait_send()
            return 0
        lax.fori_loop(1, 16, go, 0)

    feats = jnp.concatenate([pos[...], jnp.ones((1, 64), F32)] + [mom[d, ri] for d in range(2) for ri in range(2)], axis=0)
    moved = permuted(feats, perm[...])
    low = lax.broadcasted_iota(jnp.int32, (8, 128), 1) < 64
    tile = jnp.where(low, moved[:8], moved[8:])
    src[core, me_z] = tile
    tgt[me_r] = tile

    pa, pb = 0.0, 0.0
    for c in range(3):
        pc = jnp.concatenate([mom[d, ri, c : c + 1] for d in range(2) for ri in range(2)], axis=0)
        pa = pa + nn(pc, mode[0, c])
        pb = pb + nn(pc, mode[1, c])
    for d in range(2):
        re = pa[2 * d : 2 * d + 1] - pb[2 * d + 1 : 2 * d + 2]
        im = pa[2 * d + 1 : 2 * d + 2] + pb[2 * d : 2 * d + 1]
        for q in range(4):
            amp[8 * d + q] = re[:, 128 * q : 128 * q + 128]
            amp[8 * d + 4 + q] = im[:, 128 * q : 128 * q + 128]

    pl.semaphore_wait(barrier, 31)

    mine = src.at[core]
    spread_to(tgt, tgt_s, tgt_r, me_r, at_r)
    spread_to(mine, src_s, src_r, me_z, at_z)

    def scatter(s, _):
        j = (me_r + s) % 16
        remote(amp.at[j], rs.at[me_r], rs_s.at[j], rs_r.at[me_r], at_r(j)).start()
        return 0

    lax.fori_loop(1, 16, scatter, 0)
    rs[me_r] = amp[me_r]

    ox, oz, oyt = 15.5, 4.0 * zl.astype(F32) + 1.5, (16 * zh + 2 * core).astype(F32) + 6.5
    arrived(tgt, tgt_s, tgt_r, me_r, at_r)
    prep_targets(tgt, (ox, oyt, oz), me_r, ta, xrow)
    acc[...] = jnp.zeros_like(acc)

    def one_block(step, _):
        quad = (me_z // 4 + step) % 4
        away = step // 4
        from_core = (core + away) % 2
        quad_ref = src.at[from_core, pl.ds(4 * quad, 4)]

        @pl.when(away == 0)
        def _():
            def go(k, _):
                z = 4 * quad + k
                @pl.when(z != me_z)
                def _():
                    remote(mine.at[z], mine.at[z], src_s.at[z], src_r.at[z], at_z(z)).wait_recv()
                return 0
            lax.fori_loop(0, 4, go, 0)
            remote(quad_ref, quad_ref, fwd_s.at[quad], fwd_r.at[quad], sibling).start()

        @pl.when(away == 1)
        def _():
            remote(quad_ref, quad_ref, fwd_s.at[quad], fwd_r.at[quad], sibling).wait_recv()

        half = quad // 2
        oys = (16 * half + 4 * y).astype(F32) + 1.5
        own = jnp.where(step == 0, (me_z % 4) * 64, -1000)
        prep_sources(src.at[from_core], quad, (ox, oys, oz), oyt, own, emap, wmat, sb)
        for c in range(4):
            r2b[...] = jnp.dot(sb[...], ta[c], preferred_element_type=F32)
            for k in range(16):
                for n, v in enumerate(planes(r2b[16 * k : 16 * k + 16, :])):
                    h, l = split(v)
                    g[0, 256 * n + 16 * k : 256 * n + 16 * k + 16, :] = h
                    g[1, 256 * n + 16 * k : 256 * n + 16 * k + 16, :] = l
            w = wmat[c]
            acc[half, c] += jnp.dot(w, g[0], preferred_element_type=F32) + jnp.dot(w, g[1], preferred_element_type=F32)

        @pl.when(step == 1)
        def _():
            arrived(rs, rs_s, rs_r, me_r, at_r)
            zb[me_z] = jnp.sum(rs[...], axis=0)
            spread_to(zb, zb_s, zb_r, me_z, at_z)

        @pl.when(step == 4)
        def _():
            arrived(zb, zb_s, zb_r, me_z, at_z)
            cb[core] = jnp.sum(zb[...], axis=0)
            remote(cb.at[core], cb.at[core], cb_s.at[0], cb_r.at[0], sibling).start()

        @pl.when(step == 5)
        def _():
            remote(cb.at[1 - core], cb.at[1 - core], cb_s.at[0], cb_r.at[0], sibling).wait_recv()
            ag[me_r] = cb[0] + cb[1]
            spread_to(ag, ag_s, ag_r, me_r, at_r)

        return 0

    lax.fori_loop(0, 8, one_block, 0)

    lane = lax.broadcasted_iota(jnp.int32, (8, 128), 1)
    fa, fb = [], []
    for c in range(4):
        f = 0.0
        for half in range(2):
            dy = (oyt - ((16 * half + 4 * y).astype(F32) + 1.5)) * KAPPA
            f = f + finish(acc[half, c], xrow[c], dy)
        fa.append(f[:8])
        fb.append(jnp.concatenate([f[8:], jnp.zeros((4, 256), F32)], axis=0))
    for r in range(16):
        t, k = r // 8, r % 8
        v = jnp.zeros((8, 128), F32)
        for c in range(4):
            for top, rows in ((0, fa[c]), (64, fb[c])):
                a = rows[:, 128 * t : 128 * t + 128]
                shift = (top + 16 * (c - k)) % 128
                if shift:
                    a = pltpu.roll(a, shift, 1)
                v = jnp.where(lane // 16 == top // 16 + c, a, v)
        obuf[r] = v

    def give(s, _):
        j = (me_r + s) % 16
        remote(obuf.at[j], rbuf.at[me_r], o_s.at[j], o_r.at[me_r], at_r(j)).start()
        return 0

    lax.fori_loop(1, 16, give, 0)
    rbuf[me_r] = obuf[me_r]

    arrived(ag, ag_s, ag_r, me_r, at_r)
    rows = [jnp.concatenate([ag[4 * k + q] for q in range(4)], axis=1) for k in range(4)]
    den = det[...] * det[...] + wid[...] * wid[...]
    rr, ri = det[...] / den, wid[...] / den
    weighted = []
    for d in range(2):
        re, im = rows[2 * d], rows[2 * d + 1]
        weighted += [rr * re - ri * im, rr * im + ri * re]
    weighted = jnp.concatenate(weighted, axis=0)
    part = []
    for c in range(3):
        part.append((nt(weighted, mode[0, c]), nt(weighted, mode[1, c])))

    sent(tgt, tgt_s, tgt_r, me_r, at_r)
    sent(mine, src_s, src_r, me_z, at_z)
    sent(zb, zb_s, zb_r, me_z, at_z)
    sent(ag, ag_s, ag_r, me_r, at_r)

    def settle(s, _):
        j = (me_r + s) % 16
        remote(amp.at[j], rs.at[me_r], rs_s.at[j], rs_r.at[me_r], at_r(j)).wait_send()
        remote(obuf.at[j], rbuf.at[me_r], o_s.at[j], o_r.at[me_r], at_r(j)).wait_send()
        return 0

    lax.fori_loop(1, 16, settle, 0)
    remote(cb.at[core], cb.at[core], cb_s.at[0], cb_r.at[0], sibling).wait_send()

    def settle_quads(q, _):
        quad_ref = mine.at[pl.ds(4 * q, 4)]
        remote(quad_ref, quad_ref, fwd_s.at[q], fwd_r.at[q], sibling).wait_send()
        return 0

    lax.fori_loop(0, 4, settle_quads, 0)
    arrived(rbuf, o_s, o_r, me_r, at_r)
    total = jnp.sum(rbuf[...], axis=0)
    total = jnp.concatenate([total, pltpu.roll(total, 64, 1)], axis=0)[:, :64]
    field = permuted(total, unperm[...]) * (COUPLING * KAPPA)
    pr, pi = ipr[...], ipi[...]
    for d in range(2):
        for c in range(3):
            a, b = part[c]
            pre, pim = mom[d, 0, c : c + 1], mom[d, 1, c : c + 1]
            k = 6 * d + c
            mre = a[2 * d : 2 * d + 1] - b[2 * d + 1 : 2 * d + 2]
            mim = a[2 * d + 1 : 2 * d + 2] + b[2 * d : 2 * d + 1]
            out[d, 0, c : c + 1] = pr * pre - pi * pim - field[k : k + 1, :64] - mre
            out[d, 1, c : c + 1] = pr * pim + pi * pre - field[k + 3 : k + 4, :64] - mim


def on_device(positions, moments, inv_polar_re, inv_polar_im, mode_field, mode_detune, mode_width):
    table = perm_map()
    back = np.zeros((64, 128), np.float32)
    back[:, :64] = table[:, :64].T
    vm = pl.BlockSpec(memory_space=pltpu.VMEM)
    dma = lambda n: pltpu.SemaphoreType.DMA((n,))
    return pl.pallas_call(
        kernel,
        out_shape=jax.ShapeDtypeStruct(moments.shape, F32),
        in_specs=[vm] * 10,
        out_specs=vm,
        scratch_shapes=[
            pltpu.VMEM((2, 16, 8, 128), F32),
            pltpu.VMEM((16, 8, 128), F32),
            pltpu.VMEM((4, 128, 256), BF16),
            pltpu.VMEM((4, 8, 256), F32),
            pltpu.VMEM((4, 128, 1024), BF16),
            pltpu.VMEM((256, 128), BF16),
            pltpu.VMEM((2, 1024, 256), BF16),
            pltpu.VMEM((256, 256), F32),
            pltpu.VMEM((2, 4, 128, 256), F32),
            pltpu.VMEM((16, 1, 128), F32),
            pltpu.VMEM((16, 1, 128), F32),
            pltpu.VMEM((16, 1, 128), F32),
            pltpu.VMEM((2, 1, 128), F32),
            pltpu.VMEM((16, 1, 128), F32),
            pltpu.VMEM((16, 8, 128), F32),
            pltpu.VMEM((16, 8, 128), F32),
        ]
        + [dma(16), dma(16), dma(16), dma(16), dma(4), dma(4), dma(16), dma(16)]
        + [dma(16), dma(16), dma(1), dma(1), dma(16), dma(16), dma(16), dma(16)],
        compiler_params=pltpu.CompilerParams(collective_id=0, has_side_effects=True, vmem_limit_bytes=48 << 20),
    )(
        positions,
        moments,
        inv_polar_re.reshape(1, -1),
        inv_polar_im.reshape(1, -1),
        mode_field,
        mode_detune.reshape(1, -1),
        mode_width.reshape(1, -1),
        jnp.asarray(feature_maps(), BF16),
        jnp.asarray(table, BF16),
        jnp.asarray(back, BF16),
    )


def solution(mesh):
    both = ("blk", "grp")
    placed = (P(None, both), P(None, None, None, both), P(both), P(both), P(None, None, both, None), P(), P())
    return jax.shard_map(on_device, mesh=mesh, in_specs=placed, out_specs=P(None, None, None, both), check_vma=False)
```

time: 261 us -> 57.6 us (0.22)
  blocking collectives: 133 us -> 0 us
  other arithmetic: 79.1 us -> 0 us
  Pallas kernels: 0 us -> 52.9 us
  starting transfers between devices: 23.9 us -> 0 us
  waiting for transfers between devices: 14 us -> 0 us
  local copies, waits for them, and re-layouts: 7.4 us -> 4.13 us
  matrix products: 2.91 us -> 0 us
    reduce_sum x9 -> x0, other arithmetic: 76.6 us -> none  [the longest x8 76.6 us: pair_field(): jnp.sum(entry_tile, axis=axis_sum)]
    psum x5 -> x0, blocking collectives: 72.2 us -> none  [over_axes(): value = lax.psum(value, axis)]
    all_gather x2 -> x0, blocking collectives: 60.3 us -> none  [gather_in_order(): tiles = lax.all_gather(tiles, axes[k], axis=0, tiled=True)]
    pallas_call x0 -> x1, Pallas kernels: none -> 52.9 us  [on_device(): pl.pallas_call(kernel, out_shape=jax.ShapeDtypeStruct(moments.shape, F32)...]
    all_to_all x2 -> x0, starting transfers between devices: 23.9 us -> none  [the longest x1 15.9 us: sent_to_all(): lax.all_to_all(jnp.broadcast_to(value[None], (devices, *value.shape)), ax...]
    all_to_all x2 -> x0, waiting for transfers between devices: 14 us -> none  [the longest x1 14 us: sent_and_summed(): lax.all_to_all(tiles, axis, split_axis=0, concat_axis=0, tiled=True)]
    dot_general x8 -> x0, matrix products: 2.91 us -> none  [the longest x4 1.62 us: spread(): lax.dot_general(weights, rows, (((0,), (1,)), ((), ())), precision=lax.Pr...]
  transfers between devices with their start and end apart: 2 -> 0, of which waited for: 1 -> 0; matrix products, arithmetic and copies ran while one was open for 1% -> 0% of each run, Pallas kernels for 0% -> 0%
where the time goes in v1:
time: 57.6 us; the launch traced here: 57.1 us
  Pallas kernels  52.9 us (92%)
  local copies, waits for them, and re-layouts  4.13 us (7%)
    pallas_call x1, Pallas kernels, on_device(): pl.pallas_call(kernel, out_shape=jax.ShapeDtypeStruct(moments.shape, F32)...  52.9 us
    unnamed x19, local copies, waits for them, and re-layouts  3.53 us

profile of v1, /device:TPU:1, one launch (start us, length us, event | category | flops | bytes accessed | tf_op | source)
XLA Modules:
  0.0 57.1 jit_solution(11979254790819448307)
XLA Ops:
  0.0 0.0 copy-start.2
  0.0 0.0 copy-start.4
  0.0 0.0 copy-start.5
  0.0 0.0 copy-start.6
  0.0 0.0 copy-start.7
  0.0 0.0 copy-start.8
  0.0 0.7 %copy.11.mom = f32[2,2,3,64]{3,2,1,0:T(4,128)S(1)} copy(f32[2,2,3,64]{3,1,2,0:T(2,128)} %param.11) | data formatting | bytes 6144 | tf_op args[1]
  0.8 0.0 copy-done.2
  0.8 0.0 copy-done.4
  0.8 0.0 copy-done.5
  0.8 0.0 copy-done.6
  0.8 0.0 copy-done.7
  0.8 0.0 copy-done.8
  0.8 0.0 copy-start
  0.8 1.1 %copy-done = f32[2,3,64,512]{3,2,1,0:T(8,128)S(1)} copy-done((f32[2,3,64,512]{3,2,1,0:T(8,128)S(1)}, f32[2,3,64,512]{3,2,1,0:T(8,128)}, u32[]{:S(2)}) %copy-start) | copy-done | bytes 786456
  2.0 0.0 copy-start.1
  2.0 0.9 %copy-done.1 = bf16[4,160,96]{2,1,0:T(8,128)(2,1)S(1)} copy-done((bf16[4,160,96]{2,1,0:T(8,128)(2,1)S(1)}, bf16[4,160,96]{2,1,0:T(8,128)(2,1)}, u32[]{:S(2)}) %copy-start.1) | copy-done | bytes 122904
  2.9 0.0 copy-start.3
  2.9 0.7 %copy-done.3 = bf16[64,128]{1,0:T(8,128)(2,1)S(1)} copy-done((bf16[64,128]{1,0:T(8,128)(2,1)S(1)}, bf16[64,128]{1,0:T(8,128)(2,1)}, u32[]{:S(2)}) %copy-start.3) | copy-done | bytes 16408
  3.6 52.9 %shard_map.100 = f32[2,2,3,64]{3,2,1,0:T(4,128)S(1)} custom-call(f32[3,64]{1,0:T(4,128)S(1)} %copy-done.4, f32[2,2,3,64]{3,2,1,0:T(4,128)S(1)} %copy.11.mom, f32[1,64]{1,0:T(1,128)S(1)} %bitcast.6, f32[1,64]{1,0:T(1,128)S(1)} %bitcast.7, f32[2,3,64,512]{3,2,1,0:T(8,128)S(1)} %copy-done, f32[1,512]{1,0:T(1,128)S(1)} %bitcast.4, f32[1,512]{1,0:T(1,128)S(1)} %bitcast.5, ...), custom_call_target="tpu_custom_call" | custom-call | tf_op jit(solution)/shard_map/pallas_call | solution.py:436
  56.5 0.6 %copy.12 = f32[2,2,3,64]{3,1,2,0:T(2,128)} copy(f32[2,2,3,64]{3,2,1,0:T(4,128)S(1)} %shard_map.100) | data formatting | bytes 6144 | tf_op jit(solution)/shard_map/pallas_call | solution.py:436
Async XLA Ops:
  0.0 0.8 %copy-start.2 = (bf16[64,128]{1,0:T(8,128)(2,1)S(1)}, bf16[64,128]{1,0:T(8,128)(2,1)}, u32[]{:S(2)}) copy-start(bf16[64,128]{1,0:T(8,128)(2,1)} %constant.8.clone.unperm) | copy-start | bytes 49156
  0.0 0.8 %copy-start.4 = (f32[3,64]{1,0:T(4,128)S(1)}, f32[3,64]{1,0:T(4,128)}, u32[]{:S(2)}) copy-start(f32[3,64]{1,0:T(4,128)} %pos.1) | copy-start | bytes 2308
  0.0 0.8 %copy-start.5 = (f32[512]{0:T(512)S(1)}, f32[512]{0:T(512)}, u32[]{:S(2)}) copy-start(f32[512]{0:T(512)} %param.15) | copy-start | bytes 6148
  0.0 0.8 %copy-start.6 = (f32[512]{0:T(512)S(1)}, f32[512]{0:T(512)}, u32[]{:S(2)}) copy-start(f32[512]{0:T(512)} %param.16) | copy-start | bytes 6148
  0.0 0.8 %copy-start.7 = (f32[64]{0:T(128)S(1)}, f32[64]{0:T(128)}, u32[]{:S(2)}) copy-start(f32[64]{0:T(128)} %param.12) | copy-start | bytes 772
  0.0 0.8 %copy-start.8 = (f32[64]{0:T(128)S(1)}, f32[64]{0:T(128)}, u32[]{:S(2)}) copy-start(f32[64]{0:T(128)} %param.13) | copy-start | bytes 772
  0.8 1.1 %copy-start = (f32[2,3,64,512]{3,2,1,0:T(8,128)S(1)}, f32[2,3,64,512]{3,2,1,0:T(8,128)}, u32[]{:S(2)}) copy-start(f32[2,3,64,512]{3,2,1,0:T(8,128)} %mode.1) | copy-start | bytes 2359300
  2.0 0.9 %copy-start.1 = (bf16[4,160,96]{2,1,0:T(8,128)(2,1)S(1)}, bf16[4,160,96]{2,1,0:T(8,128)(2,1)}, u32[]{:S(2)}) copy-start(bf16[4,160,96]{2,1,0:T(8,128)(2,1)} %constant.6.clone.emap) | copy-start | bytes 368644
  2.9 0.7 %copy-start.3 = (bf16[64,128]{1,0:T(8,128)(2,1)S(1)}, bf16[64,128]{1,0:T(8,128)(2,1)}, u32[]{:S(2)}) copy-start(bf16[64,128]{1,0:T(8,128)(2,1)} %constant.7.clone.perm) | copy-start | bytes 49156

commit v2 on v1

--- a/solution.py
+++ b/solution.py
@@ -205,8 +205,9 @@
     return o[:n] + o[n : 2 * n] + o[2 * n :]
 
 
-def kernel(pos, mom, ipr, ipi, mode, det, wid, emap, perm, unperm, out,
-           src, tgt, ta, xrow, wmat, sb, g, r2b, acc, amp, rs, zb, cb, ag, obuf, rbuf,
+def kernel(pos_h, mom_h, ipr_h, ipi_h, mode_h, det_h, wid_h, emap_h, perm_h, unperm_h, out,
+           pos, mom, ipr, ipi, mode, det, wid, emap, perm, unperm, in_sem,
+           src, tgt, ta, xrow, wmat, sb, ga, gb, ra, rb, acc, amp, rs, zb, cb, ag, obuf, rbuf,
            tgt_s, tgt_r, src_s, src_r, fwd_s, fwd_r, rs_s, rs_r, zb_s, zb_r, cb_s, cb_r, ag_s, ag_r, o_s, o_r):
     blk, grp = lax.axis_index("blk"), lax.axis_index("grp")
     zl, x, zh, y, core = blk // 4, blk % 4, grp // 8, (grp // 2) % 4, grp % 2
@@ -227,8 +228,20 @@
         pl.semaphore_signal(barrier, inc=1, device_id=at_z((me_z + s) % 16), device_id_type=MESH)
         return 0
 
-    lax.fori_loop(1, 16, greet, 0)
+    lax.fori_loop(1, 16, greet, 0, unroll=5)
     pl.semaphore_signal(barrier, inc=1, device_id=sibling, device_id_type=MESH)
+
+    fetched = [
+        pltpu.make_async_copy(a, b, in_sem.at[k])
+        for k, (a, b) in enumerate(
+            zip(
+                (pos_h, mom_h, perm_h, mode_h, emap_h, det_h, wid_h, ipr_h, ipi_h, unperm_h),
+                (pos, mom, perm, mode, emap, det, wid, ipr, ipi, unperm),
+            )
+        )
+    ]
+    for copy in fetched:
+        copy.start()
 
     def remote(a, b, ss, rr, dev):
         return pltpu.make_async_remote_copy(src_ref=a, dst_ref=b, send_sem=ss, recv_sem=rr, device_id=dev, device_id_type=MESH)
@@ -238,7 +251,7 @@
             j = (me + s) % 16
             remote(buf.at[me], buf.at[me], ss.at[j], rr.at[me], where(j)).start()
             return 0
-        lax.fori_loop(1, 16, go, 0)
+        lax.fori_loop(1, 16, go, 0, unroll=5)
 
     def arrived(buf, ss, rr, me, where):
         def go(s, _):
@@ -254,16 +267,23 @@
             return 0
         lax.fori_loop(1, 16, go, 0)
 
-    feats = jnp.concatenate([pos[...], jnp.ones((1, 64), F32)] + [mom[d, ri] for d in range(2) for ri in range(2)], axis=0)
+    for copy in fetched[:3]:
+        copy.wait()
+    feats = jnp.concatenate(
+        [pos[...], jnp.ones((1, 64), F32)]
+        + [mom[d, c, ri : ri + 1] for d in range(2) for ri in range(2) for c in range(3)],
+        axis=0,
+    )
     moved = permuted(feats, perm[...])
     low = lax.broadcasted_iota(jnp.int32, (8, 128), 1) < 64
     tile = jnp.where(low, moved[:8], moved[8:])
     src[core, me_z] = tile
     tgt[me_r] = tile
 
+    fetched[3].wait()
     pa, pb = 0.0, 0.0
     for c in range(3):
-        pc = jnp.concatenate([mom[d, ri, c : c + 1] for d in range(2) for ri in range(2)], axis=0)
+        pc = jnp.concatenate([mom[d, c] for d in range(2)], axis=0)
         pa = pa + nn(pc, mode[0, c])
         pb = pb + nn(pc, mode[1, c])
     for d in range(2):
@@ -273,6 +293,8 @@
             amp[8 * d + q] = re[:, 128 * q : 128 * q + 128]
             amp[8 * d + 4 + q] = im[:, 128 * q : 128 * q + 128]
 
+    for copy in fetched[4:]:
+        copy.wait()
     pl.semaphore_wait(barrier, 31)
 
     mine = src.at[core]
@@ -284,13 +306,33 @@
         remote(amp.at[j], rs.at[me_r], rs_s.at[j], rs_r.at[me_r], at_r(j)).start()
         return 0
 
-    lax.fori_loop(1, 16, scatter, 0)
+    lax.fori_loop(1, 16, scatter, 0, unroll=5)
     rs[me_r] = amp[me_r]
 
     ox, oz, oyt = 15.5, 4.0 * zl.astype(F32) + 1.5, (16 * zh + 2 * core).astype(F32) + 6.5
     arrived(tgt, tgt_s, tgt_r, me_r, at_r)
     prep_targets(tgt, (ox, oyt, oz), me_r, ta, xrow)
     acc[...] = jnp.zeros_like(acc)
+    gb[...] = jnp.zeros_like(gb)
+    wmat[1, 3] = jnp.zeros((128, 1024), BF16)
+
+    def stage(w, gold, gnew, rnow, nxt, rnext):
+        total = None
+        for q in range(8):
+            ko = 256 * (q % 4)
+            part = jnp.dot(w[:, ko : ko + 256], gold[q // 4, ko : ko + 256], preferred_element_type=F32)
+            if nxt is not None and q % 4 == 0:
+                top = 32 * q
+                r2 = jnp.dot(sb[top : top + 128], ta[nxt], preferred_element_type=F32)
+            for k in (2 * q, 2 * q + 1):
+                for n, v in enumerate(planes(rnow[16 * k : 16 * k + 16, :])):
+                    h, l = split(v)
+                    gnew[0, 256 * n + 16 * k : 256 * n + 16 * k + 16, :] = h
+                    gnew[1, 256 * n + 16 * k : 256 * n + 16 * k + 16, :] = l
+            if nxt is not None and q % 4 == 0:
+                rnext[top : top + 128] = r2
+            total = part if total is None else total + part
+        return total
 
     def one_block(step, _):
         quad = (me_z // 4 + step) % 4
@@ -316,16 +358,14 @@
         half = quad // 2
         oys = (16 * half + 4 * y).astype(F32) + 1.5
         own = jnp.where(step == 0, (me_z % 4) * 64, -1000)
-        prep_sources(src.at[from_core], quad, (ox, oys, oz), oyt, own, emap, wmat, sb)
-        for c in range(4):
-            r2b[...] = jnp.dot(sb[...], ta[c], preferred_element_type=F32)
-            for k in range(16):
-                for n, v in enumerate(planes(r2b[16 * k : 16 * k + 16, :])):
-                    h, l = split(v)
-                    g[0, 256 * n + 16 * k : 256 * n + 16 * k + 16, :] = h
-                    g[1, 256 * n + 16 * k : 256 * n + 16 * k + 16, :] = l
-            w = wmat[c]
-            acc[half, c] += jnp.dot(w, g[0], preferred_element_type=F32) + jnp.dot(w, g[1], preferred_element_type=F32)
+        par = step % 2
+        prep_sources(src.at[from_core], quad, (ox, oys, oz), oyt, own, emap, wmat.at[par], sb)
+        ra[...] = jnp.dot(sb[...], ta[0], preferred_element_type=F32)
+        before = ((me_z // 4 + step + 3) % 4) // 2
+        acc[before, 3] += stage(wmat.at[1 - par, 3], gb, ga, ra, 1, rb)
+        acc[half, 0] += stage(wmat.at[par, 0], ga, gb, rb, 2, ra)
+        acc[half, 1] += stage(wmat.at[par, 1], gb, ga, ra, 3, rb)
+        acc[half, 2] += stage(wmat.at[par, 2], ga, gb, rb, None, None)
 
         @pl.when(step == 1)
         def _():
@@ -348,6 +388,9 @@
         return 0
 
     lax.fori_loop(0, 8, one_block, 0)
+    last = ((me_z // 4 + 3) % 4) // 2
+    w = wmat[1, 3]
+    acc[last, 3] += jnp.dot(w, gb[0], preferred_element_type=F32) + jnp.dot(w, gb[1], preferred_element_type=F32)
 
     lane = lax.broadcasted_iota(jnp.int32, (8, 128), 1)
     fa, fb = [], []
@@ -375,7 +418,7 @@
         remote(obuf.at[j], rbuf.at[me_r], o_s.at[j], o_r.at[me_r], at_r(j)).start()
         return 0
 
-    lax.fori_loop(1, 16, give, 0)
+    lax.fori_loop(1, 16, give, 0, unroll=5)
     rbuf[me_r] = obuf[me_r]
 
     arrived(ag, ag_s, ag_r, me_r, at_r)
@@ -419,12 +462,12 @@
     for d in range(2):
         for c in range(3):
             a, b = part[c]
-            pre, pim = mom[d, 0, c : c + 1], mom[d, 1, c : c + 1]
+            pre, pim = mom[d, c, 0:1], mom[d, c, 1:2]
             k = 6 * d + c
             mre = a[2 * d : 2 * d + 1] - b[2 * d + 1 : 2 * d + 2]
             mim = a[2 * d + 1 : 2 * d + 2] + b[2 * d : 2 * d + 1]
-            out[d, 0, c : c + 1] = pr * pre - pi * pim - field[k : k + 1, :64] - mre
-            out[d, 1, c : c + 1] = pr * pim + pi * pre - field[k + 3 : k + 4, :64] - mim
+            out[d, c, 0:1] = pr * pre - pi * pim - field[k : k + 1, :64] - mre
+            out[d, c, 1:2] = pr * pim + pi * pre - field[k + 3 : k + 4, :64] - mim
 
 
 def on_device(positions, moments, inv_polar_re, inv_polar_im, mode_field, mode_detune, mode_width):
@@ -433,19 +476,35 @@
     back[:, :64] = table[:, :64].T
     vm = pl.BlockSpec(memory_space=pltpu.VMEM)
     dma = lambda n: pltpu.SemaphoreType.DMA((n,))
-    return pl.pallas_call(
+    arrays = (
+        positions,
+        moments.transpose(0, 2, 1, 3),
+        inv_polar_re.reshape(1, -1),
+        inv_polar_im.reshape(1, -1),
+        mode_field,
+        mode_detune.reshape(1, -1),
+        mode_width.reshape(1, -1),
+        jnp.asarray(feature_maps(), BF16),
+        jnp.asarray(table, BF16),
+        jnp.asarray(back, BF16),
+    )
+    response = pl.pallas_call(
         kernel,
-        out_shape=jax.ShapeDtypeStruct(moments.shape, F32),
-        in_specs=[vm] * 10,
+        out_shape=jax.ShapeDtypeStruct(arrays[1].shape, F32),
+        in_specs=[pl.BlockSpec(memory_space=pl.ANY)] * 10,
         out_specs=vm,
-        scratch_shapes=[
+        scratch_shapes=[pltpu.VMEM(a.shape, a.dtype) for a in arrays]
+        + [
+            dma(10),
             pltpu.VMEM((2, 16, 8, 128), F32),
             pltpu.VMEM((16, 8, 128), F32),
             pltpu.VMEM((4, 128, 256), BF16),
             pltpu.VMEM((4, 8, 256), F32),
-            pltpu.VMEM((4, 128, 1024), BF16),
+            pltpu.VMEM((2, 4, 128, 1024), BF16),
             pltpu.VMEM((256, 128), BF16),
             pltpu.VMEM((2, 1024, 256), BF16),
+            pltpu.VMEM((2, 1024, 256), BF16),
+            pltpu.VMEM((256, 256), F32),
             pltpu.VMEM((256, 256), F32),
             pltpu.VMEM((2, 4, 128, 256), F32),
             pltpu.VMEM((16, 1, 128), F32),
@@ -458,19 +517,9 @@
         ]
         + [dma(16), dma(16), dma(16), dma(16), dma(4), dma(4), dma(16), dma(16)]
         + [dma(16), dma(16), dma(1), dma(1), dma(16), dma(16), dma(16), dma(16)],
-        compiler_params=pltpu.CompilerParams(collective_id=0, has_side_effects=True, vmem_limit_bytes=48 << 20),
-    )(
-        positions,
-        moments,
-        inv_polar_re.reshape(1, -1),
-        inv_polar_im.reshape(1, -1),
-        mode_field,
-        mode_detune.reshape(1, -1),
-        mode_width.reshape(1, -1),
-        jnp.asarray(feature_maps(), BF16),
-        jnp.asarray(table, BF16),
-        jnp.asarray(back, BF16),
-    )
+        compiler_params=pltpu.CompilerParams(collective_id=0, has_side_effects=True, vmem_limit_bytes=60 << 20),
+    )(*arrays)
+    return response.transpose(0, 2, 1, 3)
 
 
 def solution(mesh):

time: 57.6 us -> 54.6 us (0.948)
  local copies, waits for them, and re-layouts: 4.13 us -> 1.29 us
    unnamed x19 -> x1, local copies, waits for them, and re-layouts: 3.53 us -> 1.29 us
    pallas_call x1 -> x0, local copies, waits for them, and re-layouts: 0.6 us -> none  [on_device(): pl.pallas_call(kernel, out_shape=jax.ShapeDtypeStruct(moments.shape, F32)...]
where the time goes in v2:
time: 54.6 us; the launch traced here: 54.2 us
  Pallas kernels  52.9 us (97%)
  local copies, waits for them, and re-layouts  1.29 us (2%)
    pallas_call x1, Pallas kernels, on_device(): pl.pallas_call(kernel, out_shape=jax.ShapeDtypeStruct(arrays[1].shape, F3...  52.9 us
    unnamed x1, local copies, waits for them, and re-layouts  1.29 us

profile of v2, /device:TPU:1, one launch (start us, length us, event | category | flops | bytes accessed | tf_op | source)
XLA Modules:
  0.0 54.2 jit_solution(2235067146596795127)
XLA Ops:
  0.0 52.9 %shard_map.100 = f32[2,3,2,64]{3,2,1,0:T(2,128)} custom-call(f32[3,64]{1,0:T(4,128)} %pos_h.1, f32[2,3,2,64]{3,2,1,0:T(2,128)} %bitcast.7, f32[1,64]{1,0:T(1,128)} %bitcast.10, f32[1,64]{1,0:T(1,128)} %bitcast.11, f32[2,3,64,512]{3,2,1,0:T(8,128)} %mode_h.1, f32[1,512]{1,0:T(1,128)} %bitcast.8, f32[1,512]{1,0:T(1,128)} %bitcast.9, ...), custom_call_target="tpu_custom_call" | custom-call | tf_op jit(solution)/shard_map/pallas_call | solution.py:491
  52.9 1.3 %copy.12 = f32[2,2,3,64]{3,1,2,0:T(2,128)} copy(f32[2,2,3,64]{3,1,2,0:T(2,128)} %bitcast.6) | data formatting | bytes 6144

commit v3 on v2

--- a/solution.py
+++ b/solution.py
@@ -53,7 +53,7 @@
     return h, m, rest - m
 
 
-S4 = [4.442882834891087, -7.308241184594817, 3.6062893302761356, -0.8457653963567059, 0.10920874208169386]
+S4 = [4.442867982147176, -7.307445408741119, 3.59480206222511, -0.7844035161415288]
 C5 = [1.4142134965690698, -6.978850988398392, 5.73946117217025, -1.8835629909695983, 0.3106981907767927]
 
 def planes(r2):
@@ -66,16 +66,17 @@
     s = s * f
     c = C5[-1]
     for k in C5[-2::-1]: c = c * t + k
-    sy = s * y
-    gr = y - s * sy
+    y23 = y * (2.0 / 3.0)
+    sy = s * y23
+    gr = y23 - s * sy
     gi = sy * c
     q = y * y
-    u = y * KAPPA
-    v1 = 1.0 - q * (KAPPA * KAPPA)
+    u = y * (1.5 * KAPPA)
+    v1 = 1.5 - q * (1.5 * KAPPA * KAPPA)
     ar = gr * v1 - gi * u
     ai = gi * v1 + gr * u
-    br = q * (ar - (2.0 / 3.0) * gr)
-    bi = q * (ai - (2.0 / 3.0) * gi)
+    br = q * (ar - gr)
+    bi = q * (ai - gi)
     return ar, ai, br, bi
 
 
@@ -208,7 +209,7 @@
 def kernel(pos_h, mom_h, ipr_h, ipi_h, mode_h, det_h, wid_h, emap_h, perm_h, unperm_h, out,
            pos, mom, ipr, ipi, mode, det, wid, emap, perm, unperm, in_sem,
            src, tgt, ta, xrow, wmat, sb, ga, gb, ra, rb, acc, amp, rs, zb, cb, ag, obuf, rbuf,
-           tgt_s, tgt_r, src_s, src_r, fwd_s, fwd_r, rs_s, rs_r, zb_s, zb_r, cb_s, cb_r, ag_s, ag_r, o_s, o_r):
+           tgt_s, tgt_r, src_s, src_r, fwd_s, fwd_r, rs_s, rs_r, zb_s, zb_r, cb_s, cb_r, ag_s, ag_r, o_s, o_r, pass_s, zf_s, zf_r, zfar):
     blk, grp = lax.axis_index("blk"), lax.axis_index("grp")
     zl, x, zh, y, core = blk // 4, blk % 4, grp // 8, (grp // 2) % 4, grp % 2
     me_r, me_z = x * 4 + y, zh * 8 + zl
@@ -225,9 +226,16 @@
 
     def greet(s, _):
         pl.semaphore_signal(barrier, inc=1, device_id=at_r((me_r + s) % 16), device_id_type=MESH)
-        pl.semaphore_signal(barrier, inc=1, device_id=at_z((me_z + s) % 16), device_id_type=MESH)
-        return 0
-
+        return 0
+
+    def greet_z(s, _):
+        pl.semaphore_signal(barrier, inc=1, device_id=at_z(near(s)), device_id_type=MESH)
+        return 0
+
+    def near(s):
+        return (me_z + 12 + s + s // 4) % 16
+
+    lax.fori_loop(0, 8, greet_z, 0, unroll=4)
     lax.fori_loop(1, 16, greet, 0, unroll=5)
     pl.semaphore_signal(barrier, inc=1, device_id=sibling, device_id_type=MESH)
 
@@ -243,6 +251,8 @@
     for copy in fetched:
         copy.start()
 
+    mine = src.at[core]
+
     def remote(a, b, ss, rr, dev):
         return pltpu.make_async_remote_copy(src_ref=a, dst_ref=b, send_sem=ss, recv_sem=rr, device_id=dev, device_id_type=MESH)
 
@@ -259,6 +269,34 @@
             remote(buf.at[j], buf.at[j], ss.at[j], rr.at[j], where(j)).wait_recv()
             return 0
         lax.fori_loop(1, 16, go, 0)
+
+    def near_spread(buf, ss, rr):
+        def go(s, _):
+            z = near(s)
+            remote(buf.at[me_z], buf.at[me_z], ss.at[z], rr.at[me_z], at_z(z)).start()
+            return 0
+        lax.fori_loop(0, 8, go, 0, unroll=4)
+
+    def near_arrived(buf, ss, rr):
+        def go(s, _):
+            z = near(s)
+            remote(buf.at[z], buf.at[z], ss.at[z], rr.at[z], at_z(z)).wait_recv()
+            return 0
+        lax.fori_loop(0, 8, go, 0)
+
+    def near_sent(buf, ss, rr):
+        def go(s, _):
+            z = near(s)
+            remote(buf.at[me_z], buf.at[me_z], ss.at[z], rr.at[me_z], at_z(z)).wait_send()
+            return 0
+        lax.fori_loop(0, 8, go, 0)
+
+    up, down = (me_z + 4) % 16, (me_z + 12) % 16
+
+    def passed(k):
+        z = (me_z + jnp.where(k < 4, k + 1, 19 - k)) % 16
+        to = jnp.where(k < 4, down, up)
+        return remote(mine.at[z], mine.at[z], pass_s.at[k], src_r.at[z], at_z(to))
 
     def sent(buf, ss, rr, me, where):
         def go(s, _):
@@ -280,6 +318,11 @@
     src[core, me_z] = tile
     tgt[me_r] = tile
 
+    pl.semaphore_wait(barrier, 24)
+
+    spread_to(tgt, tgt_s, tgt_r, me_r, at_r)
+    near_spread(mine, src_s, src_r)
+
     fetched[3].wait()
     pa, pb = 0.0, 0.0
     for c in range(3):
@@ -292,14 +335,8 @@
         for q in range(4):
             amp[8 * d + q] = re[:, 128 * q : 128 * q + 128]
             amp[8 * d + 4 + q] = im[:, 128 * q : 128 * q + 128]
-
     for copy in fetched[4:]:
         copy.wait()
-    pl.semaphore_wait(barrier, 31)
-
-    mine = src.at[core]
-    spread_to(tgt, tgt_s, tgt_r, me_r, at_r)
-    spread_to(mine, src_s, src_r, me_z, at_z)
 
     def scatter(s, _):
         j = (me_r + s) % 16
@@ -310,6 +347,13 @@
     rs[me_r] = amp[me_r]
 
     ox, oz, oyt = 15.5, 4.0 * zl.astype(F32) + 1.5, (16 * zh + 2 * core).astype(F32) + 6.5
+    near_arrived(mine, src_s, src_r)
+
+    def pass_on(k, _):
+        passed(k).start()
+        return 0
+
+    lax.fori_loop(0, 7, pass_on, 0)
     arrived(tgt, tgt_s, tgt_r, me_r, at_r)
     prep_targets(tgt, (ox, oyt, oz), me_r, ta, xrow)
     acc[...] = jnp.zeros_like(acc)
@@ -335,8 +379,8 @@
         return total
 
     def one_block(step, _):
-        quad = (me_z // 4 + step) % 4
-        away = step // 4
+        quad = (me_z // 4 + step // 2) % 4
+        away = step % 2
         from_core = (core + away) % 2
         quad_ref = src.at[from_core, pl.ds(4 * quad, 4)]
 
@@ -344,7 +388,8 @@
         def _():
             def go(k, _):
                 z = 4 * quad + k
-                @pl.when(z != me_z)
+                gap = (z + 20 - me_z) % 16
+                @pl.when(gap > 8)
                 def _():
                     remote(mine.at[z], mine.at[z], src_s.at[z], src_r.at[z], at_z(z)).wait_recv()
                 return 0
@@ -361,7 +406,7 @@
         par = step % 2
         prep_sources(src.at[from_core], quad, (ox, oys, oz), oyt, own, emap, wmat.at[par], sb)
         ra[...] = jnp.dot(sb[...], ta[0], preferred_element_type=F32)
-        before = ((me_z // 4 + step + 3) % 4) // 2
+        before = ((me_z // 4 + (step + 7) // 2) % 4) // 2
         acc[before, 3] += stage(wmat.at[1 - par, 3], gb, ga, ra, 1, rb)
         acc[half, 0] += stage(wmat.at[par, 0], ga, gb, rb, 2, ra)
         acc[half, 1] += stage(wmat.at[par, 1], gb, ga, ra, 3, rb)
@@ -371,15 +416,28 @@
         def _():
             arrived(rs, rs_s, rs_r, me_r, at_r)
             zb[me_z] = jnp.sum(rs[...], axis=0)
-            spread_to(zb, zb_s, zb_r, me_z, at_z)
-
-        @pl.when(step == 4)
+            near_spread(zb, zb_s, zb_r)
+
+        @pl.when(step == 3)
         def _():
-            arrived(zb, zb_s, zb_r, me_z, at_z)
-            cb[core] = jnp.sum(zb[...], axis=0)
+            near_arrived(zb, zb_s, zb_r)
+            above = zb[(me_z + 1) % 16] + zb[(me_z + 2) % 16] + zb[(me_z + 3) % 16]
+            above = above + zb[up]
+            below = zb[(me_z + 15) % 16] + zb[(me_z + 14) % 16] + zb[(me_z + 13) % 16]
+            zfar[0] = above
+            zfar[1] = below
+            zfar[4] = above + below + zb[down] + zb[me_z]
+            remote(zfar.at[0], zfar.at[2], zf_s.at[0], zf_r.at[0], at_z(down)).start()
+            remote(zfar.at[1], zfar.at[3], zf_s.at[1], zf_r.at[1], at_z(up)).start()
+
+        @pl.when(step == 5)
+        def _():
+            remote(zfar.at[0], zfar.at[2], zf_s.at[0], zf_r.at[0], at_z(up)).wait_recv()
+            remote(zfar.at[1], zfar.at[3], zf_s.at[1], zf_r.at[1], at_z(down)).wait_recv()
+            cb[core] = zfar[2] + zfar[3] + zfar[4]
             remote(cb.at[core], cb.at[core], cb_s.at[0], cb_r.at[0], sibling).start()
 
-        @pl.when(step == 5)
+        @pl.when(step == 6)
         def _():
             remote(cb.at[1 - core], cb.at[1 - core], cb_s.at[0], cb_r.at[0], sibling).wait_recv()
             ag[me_r] = cb[0] + cb[1]
@@ -435,8 +493,16 @@
         part.append((nt(weighted, mode[0, c]), nt(weighted, mode[1, c])))
 
     sent(tgt, tgt_s, tgt_r, me_r, at_r)
-    sent(mine, src_s, src_r, me_z, at_z)
-    sent(zb, zb_s, zb_r, me_z, at_z)
+    near_sent(mine, src_s, src_r)
+    near_sent(zb, zb_s, zb_r)
+
+    def pass_done(k, _):
+        passed(k).wait_send()
+        return 0
+
+    lax.fori_loop(0, 7, pass_done, 0)
+    remote(zfar.at[0], zfar.at[2], zf_s.at[0], zf_r.at[0], at_z(down)).wait_send()
+    remote(zfar.at[1], zfar.at[3], zf_s.at[1], zf_r.at[1], at_z(up)).wait_send()
     sent(ag, ag_s, ag_r, me_r, at_r)
 
     def settle(s, _):
@@ -516,7 +582,8 @@
             pltpu.VMEM((16, 8, 128), F32),
         ]
         + [dma(16), dma(16), dma(16), dma(16), dma(4), dma(4), dma(16), dma(16)]
-        + [dma(16), dma(16), dma(1), dma(1), dma(16), dma(16), dma(16), dma(16)],
+        + [dma(16), dma(16), dma(1), dma(1), dma(16), dma(16), dma(16), dma(16)]
+        + [dma(7), dma(2), dma(2), pltpu.VMEM((5, 1, 128), F32)],
         compiler_params=pltpu.CompilerParams(collective_id=0, has_side_effects=True, vmem_limit_bytes=60 << 20),
     )(*arrays)
     return response.transpose(0, 2, 1, 3)

time: 54.6 us -> 52.7 us (0.965)
  Pallas kernels: 52.9 us -> 50.9 us
    pallas_call x1, Pallas kernels: 52.9 us -> 50.9 us  [on_device(): pl.pallas_call(kernel, out_shape=jax.ShapeDtypeStruct(arrays[1].shape, F3...]
where the time goes in v3:
time: 52.7 us; the launch traced here: 52.2 us
  Pallas kernels  50.9 us (97%)
  local copies, waits for them, and re-layouts  1.29 us (2%)
    pallas_call x1, Pallas kernels, on_device(): pl.pallas_call(kernel, out_shape=jax.ShapeDtypeStruct(arrays[1].shape, F3...  50.9 us
    unnamed x1, local copies, waits for them, and re-layouts  1.29 us

profile of v3, /device:TPU:1, one launch (start us, length us, event | category | flops | bytes accessed | tf_op | source)
XLA Modules:
  0.0 52.2 jit_solution(1352091656080347410)
XLA Ops:
  0.0 50.9 %shard_map.100 = f32[2,3,2,64]{3,2,1,0:T(2,128)} custom-call(f32[3,64]{1,0:T(4,128)} %pos_h.1, f32[2,3,2,64]{3,2,1,0:T(2,128)} %bitcast.7, f32[1,64]{1,0:T(1,128)} %bitcast.10, f32[1,64]{1,0:T(1,128)} %bitcast.11, f32[2,3,64,512]{3,2,1,0:T(8,128)} %mode_h.1, f32[1,512]{1,0:T(1,128)} %bitcast.8, f32[1,512]{1,0:T(1,128)} %bitcast.9, ...), custom_call_target="tpu_custom_call" | custom-call | tf_op jit(solution)/shard_map/pallas_call | solution.py:557
  50.9 1.3 %copy.12 = f32[2,2,3,64]{3,1,2,0:T(2,128)} copy(f32[2,2,3,64]{3,1,2,0:T(2,128)} %bitcast.6) | data formatting | bytes 6144

commit v4 on v3

--- a/solution.py
+++ b/solution.py
@@ -222,23 +222,6 @@
 
     sibling = (blk, zh * 8 + y * 2 + (1 - core))
 
-    barrier = pltpu.get_barrier_semaphore()
-
-    def greet(s, _):
-        pl.semaphore_signal(barrier, inc=1, device_id=at_r((me_r + s) % 16), device_id_type=MESH)
-        return 0
-
-    def greet_z(s, _):
-        pl.semaphore_signal(barrier, inc=1, device_id=at_z(near(s)), device_id_type=MESH)
-        return 0
-
-    def near(s):
-        return (me_z + 12 + s + s // 4) % 16
-
-    lax.fori_loop(0, 8, greet_z, 0, unroll=4)
-    lax.fori_loop(1, 16, greet, 0, unroll=5)
-    pl.semaphore_signal(barrier, inc=1, device_id=sibling, device_id_type=MESH)
-
     fetched = [
         pltpu.make_async_copy(a, b, in_sem.at[k])
         for k, (a, b) in enumerate(
@@ -251,6 +234,24 @@
     for copy in fetched:
         copy.start()
 
+    barrier = pltpu.get_barrier_semaphore()
+
+    def greet(s, _):
+        pl.semaphore_signal(barrier, inc=1, device_id=at_r((me_r + s) % 16), device_id_type=MESH)
+        return 0
+
+    def greet_z(s, _):
+        pl.semaphore_signal(barrier, inc=1, device_id=at_z(near(s)), device_id_type=MESH)
+        return 0
+
+    def near(s):
+        return (me_z + 12 + s + s // 4) % 16
+
+    lax.fori_loop(0, 8, greet_z, 0, unroll=4)
+    lax.fori_loop(1, 16, greet, 0, unroll=5)
+    pl.semaphore_signal(barrier, inc=1, device_id=sibling, device_id_type=MESH)
+
+
     mine = src.at[core]
 
     def remote(a, b, ss, rr, dev):
@@ -259,16 +260,13 @@
     def spread_to(buf, ss, rr, me, where):
         def go(s, _):
             j = (me + s) % 16
-            remote(buf.at[me], buf.at[me], ss.at[j], rr.at[me], where(j)).start()
+            remote(buf.at[me], buf.at[me], ss.at[0], rr.at[0], where(j)).start()
             return 0
         lax.fori_loop(1, 16, go, 0, unroll=5)
 
     def arrived(buf, ss, rr, me, where):
-        def go(s, _):
-            j = (me + s) % 16
-            remote(buf.at[j], buf.at[j], ss.at[j], rr.at[j], where(j)).wait_recv()
-            return 0
-        lax.fori_loop(1, 16, go, 0)
+        many = buf.at[pl.ds(0, 15)]
+        remote(many, many, ss.at[0], rr.at[0], where((me + 1) % 16)).wait_recv()
 
     def near_spread(buf, ss, rr):
         def go(s, _):
@@ -299,11 +297,8 @@
         return remote(mine.at[z], mine.at[z], pass_s.at[k], src_r.at[z], at_z(to))
 
     def sent(buf, ss, rr, me, where):
-        def go(s, _):
-            j = (me + s) % 16
-            remote(buf.at[me], buf.at[me], ss.at[j], rr.at[me], where(j)).wait_send()
-            return 0
-        lax.fori_loop(1, 16, go, 0)
+        many = buf.at[pl.ds(0, 15)]
+        remote(many, many, ss.at[0], rr.at[0], where((me + 1) % 16)).wait_send()
 
     for copy in fetched[:3]:
         copy.wait()
@@ -340,7 +335,7 @@
 
     def scatter(s, _):
         j = (me_r + s) % 16
-        remote(amp.at[j], rs.at[me_r], rs_s.at[j], rs_r.at[me_r], at_r(j)).start()
+        remote(amp.at[j], rs.at[me_r], rs_s.at[0], rs_r.at[0], at_r(j)).start()
         return 0
 
     lax.fori_loop(1, 16, scatter, 0, unroll=5)
@@ -473,7 +468,7 @@
 
     def give(s, _):
         j = (me_r + s) % 16
-        remote(obuf.at[j], rbuf.at[me_r], o_s.at[j], o_r.at[me_r], at_r(j)).start()
+        remote(obuf.at[j], rbuf.at[me_r], o_s.at[0], o_r.at[0], at_r(j)).start()
         return 0
 
     lax.fori_loop(1, 16, give, 0, unroll=5)
@@ -505,13 +500,8 @@
     remote(zfar.at[1], zfar.at[3], zf_s.at[1], zf_r.at[1], at_z(up)).wait_send()
     sent(ag, ag_s, ag_r, me_r, at_r)
 
-    def settle(s, _):
-        j = (me_r + s) % 16
-        remote(amp.at[j], rs.at[me_r], rs_s.at[j], rs_r.at[me_r], at_r(j)).wait_send()
-        remote(obuf.at[j], rbuf.at[me_r], o_s.at[j], o_r.at[me_r], at_r(j)).wait_send()
-        return 0
-
-    lax.fori_loop(1, 16, settle, 0)
+    sent(amp, rs_s, rs_r, me_r, at_r)
+    sent(obuf, o_s, o_r, me_r, at_r)
     remote(cb.at[core], cb.at[core], cb_s.at[0], cb_r.at[0], sibling).wait_send()
 
     def settle_quads(q, _):

time: 52.7 us -> 52.3 us (level)
  no operation moved by 1% of the time
where the time goes in v4:
time: 52.3 us; the launch traced here: 51.8 us
  Pallas kernels  50.5 us (97%)
  local copies, waits for them, and re-layouts  1.29 us (2%)
    pallas_call x1, Pallas kernels, on_device(): pl.pallas_call(kernel, out_shape=jax.ShapeDtypeStruct(arrays[1].shape, F3...  50.5 us
    unnamed x1, local copies, waits for them, and re-layouts  1.29 us

profile of v4, /device:TPU:1, one launch (start us, length us, event | category | flops | bytes accessed | tf_op | source)
XLA Modules:
  0.0 51.8 jit_solution(426041743776083315)
XLA Ops:
  0.0 50.5 %shard_map.100 = f32[2,3,2,64]{3,2,1,0:T(2,128)} custom-call(f32[3,64]{1,0:T(4,128)} %pos_h.1, f32[2,3,2,64]{3,2,1,0:T(2,128)} %bitcast.7, f32[1,64]{1,0:T(1,128)} %bitcast.10, f32[1,64]{1,0:T(1,128)} %bitcast.11, f32[2,3,64,512]{3,2,1,0:T(8,128)} %mode_h.1, f32[1,512]{1,0:T(1,128)} %bitcast.8, f32[1,512]{1,0:T(1,128)} %bitcast.9, ...), custom_call_target="tpu_custom_call" | custom-call | tf_op jit(solution)/shard_map/pallas_call | solution.py:547
  50.5 1.3 %copy.12 = f32[2,2,3,64]{3,1,2,0:T(2,128)} copy(f32[2,2,3,64]{3,1,2,0:T(2,128)} %bitcast.6) | data formatting | bytes 6144

commit v5 on v4

--- a/solution.py
+++ b/solution.py
@@ -313,6 +313,9 @@
     src[core, me_z] = tile
     tgt[me_r] = tile
 
+    acc[...] = jnp.zeros_like(acc)
+    gb[...] = jnp.zeros_like(gb)
+    wmat[1, 3] = jnp.zeros((128, 1024), BF16)
     pl.semaphore_wait(barrier, 24)
 
     spread_to(tgt, tgt_s, tgt_r, me_r, at_r)
@@ -348,12 +351,9 @@
         passed(k).start()
         return 0
 
-    lax.fori_loop(0, 7, pass_on, 0)
+    lax.fori_loop(0, 7, pass_on, 0, unroll=7)
     arrived(tgt, tgt_s, tgt_r, me_r, at_r)
     prep_targets(tgt, (ox, oyt, oz), me_r, ta, xrow)
-    acc[...] = jnp.zeros_like(acc)
-    gb[...] = jnp.zeros_like(gb)
-    wmat[1, 3] = jnp.zeros((128, 1024), BF16)
 
     def stage(w, gold, gnew, rnow, nxt, rnext):
         total = None

time: 52.3 us -> 52.2 us (level)
  no operation moved by 1% of the time
where the time goes in v5:
time: 52.2 us; the launch traced here: 51.7 us
  Pallas kernels  50.4 us (97%)
  local copies, waits for them, and re-layouts  1.29 us (2%)
    pallas_call x1, Pallas kernels, on_device(): pl.pallas_call(kernel, out_shape=jax.ShapeDtypeStruct(arrays[1].shape, F3...  50.4 us
    unnamed x1, local copies, waits for them, and re-layouts  1.29 us

profile of v5, /device:TPU:1, one launch (start us, length us, event | category | flops | bytes accessed | tf_op | source)
XLA Modules:
  0.0 51.7 jit_solution(7383759937795797624)
XLA Ops:
  0.0 50.4 %shard_map.100 = f32[2,3,2,64]{3,2,1,0:T(2,128)} custom-call(f32[3,64]{1,0:T(4,128)} %pos_h.1, f32[2,3,2,64]{3,2,1,0:T(2,128)} %bitcast.7, f32[1,64]{1,0:T(1,128)} %bitcast.10, f32[1,64]{1,0:T(1,128)} %bitcast.11, f32[2,3,64,512]{3,2,1,0:T(8,128)} %mode_h.1, f32[1,512]{1,0:T(1,128)} %bitcast.8, f32[1,512]{1,0:T(1,128)} %bitcast.9, ...), custom_call_target="tpu_custom_call" | custom-call | tf_op jit(solution)/shard_map/pallas_call | solution.py:547
  50.4 1.3 %copy.12 = f32[2,2,3,64]{3,1,2,0:T(2,128)} copy(f32[2,2,3,64]{3,1,2,0:T(2,128)} %bitcast.6) | data formatting | bytes 6144
